TPU v7x, 128 devices: a whole 4x4x4 slice. The times are simulated.
128 devices in a mesh: pipe: 4 (over z_hi, core), expert: 32 (over z_lo, x, y).
Axes of the slice: x: 4, y: 4, z: 4 (z_hi: 2, z_lo: 2; z = z_hi * 2 + z_lo), core: 2. Of those that a mesh axis runs over, the one named last changes fastest.
Arguments:
- out_grad: bfloat16 [32768, 7168], P(('pipe', 'expert')), may hold values from -0.29882812 to 0.29882812
- routes: int32 [32768, 1], P(('pipe', 'expert')), may hold values from 0 to 3; in each aligned block of 256 rows (0 to 255, 256 to 511, ...) at most 128 rows name the same one
- saved_hidden: bfloat16 [4, 32, 32, 128, 1024], P('pipe', 'expert'), may hold values from -6 to 6
- master: float32 [4, 32, 512, 896], P('pipe', 'expert'), may hold values from -4 to 4
- moment1: float32 [4, 32, 512, 896], P('pipe', 'expert'), may hold values from -3 to 3
- moment2: float32 [4, 32, 512, 896], P('pipe', 'expert'), may hold values from 0.05 to 4
Outputs:
- new_master: float32 [4, 32, 512, 896], P('pipe', 'expert')
- new_moment1: float32 [4, 32, 512, 896], P('pipe', 'expert')
- new_moment2: float32 [4, 32, 512, 896], P('pipe', 'expert')
Inputs may be any that keep to these rules, and one draw needn't show every extreme that they name: `routes`: among the 256 slots of one device no expert is named more than 128 times; on some devices one expert is named exactly 128 times.
All inputs are finite; a program needn't handle non-finite values.
Results may differ from a plain program's by a relative error of at most 0.0003.
Values may be sent and summed in bfloat16 or wider, within the bound.
A program may use at most 128 MiB of HBM per device.

v0:
```python
import jax
import jax.numpy as jnp
from jax import lax
from jax.sharding import PartitionSpec as P

EXPG = 4


def partner(block, axis, stride):
    count = lax.axis_size(axis)
    route = []
    for low in range(count):
        high = low | 1 << stride
        if high != low and high < count:
            route += [(low, high), (high, low)]
    return lax.ppermute(block, axis, route)


def body(out_grad, routes, saved_hidden, master, moment1, moment2):
    expert_count = lax.axis_size("expert")
    pipe_count = lax.axis_size("pipe")
    slot_count, width = out_grad.shape
    capacity = saved_hidden.shape[3]
    hidden = saved_hidden.shape[4]
    column_split = expert_count // EXPG
    col_width = width // column_split
    route_ids = routes[:, 0]
    chosen = (route_ids[:, None] == jnp.arange(EXPG, dtype=jnp.int32)[None, :]).astype(jnp.int32)
    earlier = jnp.cumsum(chosen, axis=0) - chosen
    slot_rank = jnp.sum(earlier * chosen, axis=1)
    flat_slot = route_ids * capacity + slot_rank
    slot_ids = jnp.arange(EXPG * capacity, dtype=jnp.int32)
    matches = (flat_slot[None, :] == slot_ids[:, None]).astype(jnp.int32)
    source_row = jnp.sum(matches * jnp.arange(slot_count, dtype=jnp.int32)[None, :], axis=1)
    live_slot = jnp.sum(matches, axis=1).astype(jnp.bfloat16)
    picked = jnp.take(out_grad, source_row, axis=0) * live_slot[:, None]
    outbound = (
        picked.reshape(EXPG, capacity, column_split, col_width)
        .transpose(0, 2, 1, 3)
        .reshape(expert_count, capacity, col_width)
    )
    hidden_rows = saved_hidden.reshape(expert_count * capacity, hidden)
    arrived = lax.all_to_all(outbound, "expert", split_axis=0, concat_axis=0, tiled=True)
    flat_cols = arrived.reshape(expert_count * capacity, arrived.shape[2])
    gradient = lax.dot_general(
        hidden_rows, flat_cols, (((0,), (0,)), ((), ())), preferred_element_type=jnp.float32
    )
    pipe_index = lax.axis_index("pipe")
    keep_high = (pipe_index >= pipe_count // 2).astype(jnp.int32)
    half_rows = hidden // 2
    own_start = half_rows * keep_high
    other_start = half_rows - own_start
    own_part = lax.dynamic_slice_in_dim(gradient, own_start, half_rows, 0)
    outgoing = lax.dynamic_slice_in_dim(gradient, other_start, half_rows, 0)
    bit_total = pipe_count.bit_length() - 1
    bit_order = list(range(bit_total))
    for bit_number in bit_order:
        outgoing = partner(outgoing, "pipe", bit_number)
    summed = (own_part + outgoing)[None, None]
    new_moment1 = 0.9 * moment1 + 0.1 * summed
    new_moment2 = 0.95 * moment2 + 0.05 * summed * summed
    update = new_moment1 / (1.0 - 0.9**10) / (jnp.sqrt(new_moment2 / (1.0 - 0.95**10)) + 1e-08)
    new_master = master - 0.2 * (update + 0.05 * master)
    return (new_master, new_moment1, new_moment2)


def solution(mesh):
    in_specs = (
        P(("pipe", "expert"), None),
        P(("pipe", "expert"), None),
        P("pipe", "expert", None, None, None),
        P("pipe", "expert", None, None),
        P("pipe", "expert", None, None),
        P("pipe", "expert", None, None),
    )
    out_specs = (
        P("pipe", "expert", None, None),
        P("pipe", "expert", None, None),
        P("pipe", "expert", None, None),
    )
    return jax.shard_map(body, mesh=mesh, in_specs=in_specs, out_specs=out_specs, check_vma=False)
```

profile of v0, /device:TPU:2, one launch (start us, length us, event | category | flops | bytes accessed | tf_op | source)
XLA Modules:
  0.0 222.0 jit_solution(7720921020536434596)
XLA Ops:
  0.6 0.7 compare_convert_fusion
  1.3 1.2 reduce-window.6
  2.5 0.1 slice.10
  2.6 0.1 copy.29
  2.7 0.1 copy.30
  2.8 0.1 add_bitcast_fusion
  2.9 0.7 fusion.5
  3.6 0.7 multiply_add_fusion
  4.3 0.2 convert_reduce_fusion
  4.6 16.3 %gather_fusion = bf16[512,7168]{1,0:T(8,128)(2,1)} fusion(bf16[256,7168]{1,0:T(8,128)(2,1)} %param.6, s32[1024]{0:T(1024)S(1)} %pad_clamp_fusion), kind=kCustom, calls=%fused_computation | custom fusion | bytes 14682112 | tf_op jit(solution)/shard_map/jit(_take)/gather | solution.py:36
  20.9 4.8 %copy.39 = bf16[64,8,8,896]{3,2,1,0:T(8,128)(2,1)S(1)} copy(bf16[64,8,8,896]{3,1,2,0:T(8,128)(2,1)} %bitcast.57) | data formatting | bytes 14680064
  25.7 5.0 %fusion = bf16[4,128,8,896]{3,1,2,0:T(8,128)(2,1)} fusion(bf16[4,128,8,896]{3,2,1,0:T(8,128)(2,1)S(1)} %bitcast.59, pred[4,128]{1,0:T(4,128)(4,1)S(1)} %compare_and_fusion, bf16[4,128]{1,0:T(4,128)(2,1)S(1)} %convert_bitcast_fusion), kind=kLoop, calls=%fused_computation.2 | loop fusion | flops 7340032 | bytes 14681600 | tf_op jit(solution)/shard_map/mul | solution.py:36
  30.7 9.0 %all-to-all-start = ((bf16[32,128,896]{2,1,0:T(8,128)(2,1)}), bf16[32,128,896]{2,1,0:T(8,128)(2,1)}, u32[]{:S(2)}, u32[]{:S(2)}) async-start(bf16[32,128,896]{2,1,0:T(8,128)(2,1)} %bitcast.58), calls=%async_computation | async-start | bytes 14680064 | tf_op jit(solution)/shard_map/all_to_all | solution.py:43
  39.8 106.5 %all-to-all-done = bf16[32,128,896]{2,1,0:T(8,128)(2,1)} async-done(((bf16[32,128,896]{2,1,0:T(8,128)(2,1)}), bf16[32,128,896]{2,1,0:T(8,128)(2,1)}, u32[]{:S(2)}, u32[]{:S(2)}) %all-to-all-start) | async-done | bytes 7340064 | tf_op jit(solution)/shard_map/all_to_all | solution.py:43
  146.3 11.6 %fusion.7 = f32[896,1024]{1,0:T(8,128)S(1)} fusion(bf16[4096,896]{1,0:T(8,128)(2,1)} %bitcast.10, bf16[4096,1024]{1,0:T(8,128)(2,1)} %bitcast.66), kind=kOutput, calls=%fused_computation.26 | convolution fusion | flops 7516192768 | bytes 19398656 | tf_op jit(solution)/shard_map/dot_general | solution.py:45
  157.9 0.0 copy-start.1
  157.9 0.2 dynamic-slice_bitcast_fusion
  158.2 1.6 copy-done.1
  159.7 0.0 collective-permute-start
  159.7 3.9 %collective-permute-done = f32[512,896]{0,1:T(8,128)} collective-permute-done((f32[512,896]{0,1:T(8,128)S(1)}, f32[512,896]{0,1:T(8,128)}, u32[]{:S(2)}, u32[]{:S(2)}) %collective-permute-start) | collective-permute-done | bytes 1835040 | tf_op jit(solution)/shard_map/ppermute | solution.py:16
  163.7 3.6 %collective-permute-start.1 = (f32[512,896]{0,1:T(8,128)}, f32[512,896]{0,1:T(8,128)}, u32[]{:S(2)}, u32[]{:S(2)}) collective-permute-start(f32[512,896]{0,1:T(8,128)} %collective-permute-done), channel_id=1, source_target_pairs={{0,64},{64,0},{32,96},{96,32},{1,65},{65,1},{33,97},{97,33},{2,66}... | collective-permute-start | bytes 5505032 | tf_op jit(solution)/shard_map/ppermute | solution.py:16
  167.2 1.8 copy.28
  169.1 2.7 %copy.32 = f32[1,1,512,896]{2,3,1,0:T(8,128)} copy(f32[1,1,512,896]{3,2,1,0:T(8,128)} %param.11) | data formatting | bytes 3670016 | tf_op args[5]
  171.8 2.7 %copy.34 = f32[1,1,512,896]{2,3,1,0:T(8,128)} copy(f32[1,1,512,896]{3,2,1,0:T(8,128)} %param.9) | data formatting | bytes 3670016 | tf_op args[3]
  174.5 33.4 %collective-permute-done.1 = f32[512,896]{0,1:T(8,128)} collective-permute-done((f32[512,896]{0,1:T(8,128)}, f32[512,896]{0,1:T(8,128)}, u32[]{:S(2)}, u32[]{:S(2)}) %collective-permute-start.1) | collective-permute-done | bytes 1835040 | tf_op jit(solution)/shard_map/ppermute | solution.py:16
  207.9 6.8 %multiply_subtract_fusion = (f32[1,1,512,896]{2,3,1,0:T(8,128)}, f32[1,1,512,896]{2,3,1,0:T(8,128)}, f32[1,1,512,896]{2,3,1,0:T(8,128)}) fusion(f32[1,1,512,896]{2,3,1,0:T(8,128)} %copy.34, f32[512,896]{0,1:T(8,128)} %collective-permute-done.1, f32[896,1024]{1,0:T(8,128)} %copy-done.1, s32[]{:T(128)S(6)} %mul.82, f32[1,1,512,896]{2,3,1,0:T(8,128)S(1)} %copy.28, ...), kind=kLoop, calls=%fused_computation.8 | loop fusion | flops 7340032 | bytes 14680068 | tf_op jit(solution)/shard_map/sub | solution.py:63
  214.7 2.7 %copy.35 = f32[1,1,512,896]{3,2,1,0:T(8,128)} copy(f32[1,1,512,896]{2,3,1,0:T(8,128)} %get-tuple-element.14) | data formatting | bytes 3670016
  217.4 0.0 copy-start
  217.4 2.9 %copy.36 = f32[1,1,512,896]{3,2,1,0:T(8,128)} copy(f32[1,1,512,896]{2,3,1,0:T(8,128)} %get-tuple-element.15) | data formatting | bytes 3670016
  220.3 0.0 copy-done
  220.3 1.7 copy.37
  (6 shorter events, 0.1 us)
Async XLA Ops:
  30.7 115.6 %all-to-all-start = ((bf16[32,128,896]{2,1,0:T(8,128)(2,1)}), bf16[32,128,896]{2,1,0:T(8,128)(2,1)}, u32[]{:S(2)}, u32[]{:S(2)}) async-start(bf16[32,128,896]{2,1,0:T(8,128)(2,1)} %bitcast.58), calls=%async_computation | async-start | bytes 14680064 | tf_op jit(solution)/shard_map/all_to_all | solution.py:43
  157.9 1.8 copy-start.1
  159.7 3.9 %collective-permute-start = (f32[512,896]{0,1:T(8,128)S(1)}, f32[512,896]{0,1:T(8,128)}, u32[]{:S(2)}, u32[]{:S(2)}) collective-permute-start(f32[512,896]{0,1:T(8,128)S(1)} %dynamic-slice_bitcast_fusion), channel_id=1, source_target_pairs={{0,32},{32,0},{64,96},{96,64},{1,33},{33,1},{65,97},{97,65},{2,34}... | collective-permute-start | bytes 5505032 | tf_op jit(solution)/shard_map/ppermute | solution.py:16
  163.7 44.2 %collective-permute-start.1 = (f32[512,896]{0,1:T(8,128)}, f32[512,896]{0,1:T(8,128)}, u32[]{:S(2)}, u32[]{:S(2)}) collective-permute-start(f32[512,896]{0,1:T(8,128)} %collective-permute-done), channel_id=1, source_target_pairs={{0,64},{64,0},{32,96},{96,32},{1,65},{65,1},{33,97},{97,33},{2,66}... | collective-permute-start | bytes 5505032 | tf_op jit(solution)/shard_map/ppermute | solution.py:16
  217.4 2.9 %copy-start = (f32[1,1,512,896]{2,3,1,0:T(8,128)S(1)}, f32[1,1,512,896]{2,3,1,0:T(8,128)}, u32[]{:S(2)}) copy-start(f32[1,1,512,896]{2,3,1,0:T(8,128)} %get-tuple-element.16) | copy-start | bytes 5505028
where the time goes:
time: 222 us
  waiting for transfers between devices  144 us (65%)
  local copies, waits for them, and re-layouts  37.6 us (17%)
  other arithmetic  15.5 us (7%)
  starting transfers between devices  12.6 us (6%)
  matrix products  11.6 us (5%)
    all_to_all x1, waiting for transfers between devices, body(): lax.all_to_all(outbound, 'expert', split_axis=0, concat_axis=0, tiled=True)  107 us
    ppermute x2, waiting for transfers between devices, partner(): return lax.ppermute(block, axis, route)  37.3 us
    unnamed x11, local copies, waits for them, and re-layouts  20.8 us
    gather x1, local copies, waits for them, and re-layouts, body(): picked = jnp.take(out_grad, source_row, axis=0) * live_slot[:, None]  16.3 us
    dot_general x1, matrix products, body(): lax.dot_general(hidden_rows, flat_cols, (((0,), (0,)), ((), ())), preferr...  11.6 us
    all_to_all x1, starting transfers between devices, body(): lax.all_to_all(outbound, 'expert', split_axis=0, concat_axis=0, tiled=True)  9.03 us
    sub x1, other arithmetic, body(): new_master = master - 0.2 * (update + 0.05 * master)  6.83 us
    mul x1, other arithmetic, body(): picked = jnp.take(out_grad, source_row, axis=0) * live_slot[:, None]  5.05 us
  transfers between devices with their start and end apart: 3, of which 3 were waited for; matrix products, arithmetic and copies ran while one was open for 3% of the time, Pallas kernels for 0%

commit v1 on v0

v1 whole, which is shorter than its diff:
```python
import functools

import jax
import jax.numpy as jnp
from jax import lax
from jax.experimental import pallas as pl
from jax.experimental.pallas import tpu as pltpu
from jax.sharding import PartitionSpec as P

EXPG = 4
LANE = 128
MESH = pl.DeviceIdType.MESH


def exchange_kernel(
    grad_hbm, routes_ref, hidden_hbm, total_hbm,
    grad, place, outbound, arrived, hidden, hidden_t, own, other, code, code_in, scale, scale_in, total,
    load_sem, local_sem, send_sem, recv_sem, code_send, code_recv, scale_send, scale_recv, store_sem,
):
    pipe, me = lax.axis_index("pipe"), lax.axis_index("expert")
    pipe_count, expert_count = lax.axis_size("pipe"), lax.axis_size("expert")
    chunks, _, cap, _ = outbound.shape
    slots, width = grad.shape
    split = expert_count // EXPG
    slab = width // split
    hid = hidden_t.shape[0]
    half = hid // 2
    mirror = pipe_count - 1 - pipe
    keep_high = pipe // (pipe_count // 2)
    own_start = pl.multiple_of(keep_high * half, half)
    other_start = pl.multiple_of((1 - keep_high) * half, half)
    tile = half // 2

    load_grad = pltpu.make_async_copy(grad_hbm, grad, load_sem.at[0])
    load_grad.start()
    load_hidden = pltpu.make_async_copy(hidden_hbm.at[0, 0], hidden, load_sem.at[1])
    load_hidden.start()

    barrier = pltpu.get_barrier_semaphore()

    def greet(step, carry):
        pl.semaphore_signal(
            barrier, inc=1, device_id=(pipe, lax.rem(me + step, expert_count)), device_id_type=MESH
        )
        return carry

    lax.fori_loop(1, expert_count, greet, 0)
    pl.semaphore_signal(barrier, inc=1, device_id=(mirror, me), device_id_type=MESH)

    route = routes_ref[...]
    chosen = jnp.broadcast_to(route, (8, slots)) == lax.broadcasted_iota(jnp.int32, (8, slots), 0)
    earlier = lax.broadcasted_iota(jnp.int32, (slots, slots), 0) < lax.broadcasted_iota(jnp.int32, (slots, slots), 1)
    before = jnp.dot(
        chosen.astype(jnp.bfloat16), earlier.astype(jnp.bfloat16), preferred_element_type=jnp.float32
    )
    rank = jnp.sum(jnp.where(chosen, before, 0.0), axis=0, keepdims=True).astype(jnp.int32)
    flat = jnp.broadcast_to(route * cap + rank, (EXPG * cap, slots))
    placed = flat == lax.broadcasted_iota(jnp.int32, (EXPG * cap, slots), 0)
    place[...] = placed.astype(jnp.bfloat16)

    load_grad.wait()

    def pick(chunk):
        def one(j, carry):
            start = pl.multiple_of(j * slab + chunk * LANE, LANE)
            picked = jnp.dot(place[...], grad[:, pl.ds(start, LANE)], preferred_element_type=jnp.float32)
            picked = picked.astype(jnp.bfloat16)
            for k in range(EXPG):
                outbound[chunk, k * split + j] = picked[k * cap:(k + 1) * cap]
            return carry

        lax.fori_loop(0, split, one, 0)

    def block(chunk, peer):
        return pltpu.make_async_remote_copy(
            src_ref=outbound.at[chunk, peer],
            dst_ref=arrived.at[chunk, me],
            send_sem=send_sem.at[chunk],
            recv_sem=recv_sem.at[chunk],
            device_id=(pipe, peer),
            device_id_type=MESH,
        )

    def local(chunk):
        return pltpu.make_async_copy(outbound.at[chunk, me], arrived.at[chunk, me], local_sem.at[chunk])

    def send(chunk):
        def one(step, carry):
            block(chunk, lax.rem(me + step, expert_count)).start()
            return carry

        lax.fori_loop(1, expert_count, one, 0)
        local(chunk).start()

    def all_blocks(chunk):
        others = pl.ds(0, expert_count - 1)
        return pltpu.make_async_remote_copy(
            src_ref=outbound.at[chunk, others],
            dst_ref=arrived.at[chunk, others],
            send_sem=send_sem.at[chunk],
            recv_sem=recv_sem.at[chunk],
            device_id=(pipe, me),
            device_id_type=MESH,
        )

    pick(0)
    pl.semaphore_wait(barrier, expert_count)
    send(0)

    def pick_send(chunk, carry):
        pick(chunk)
        send(chunk)
        return carry

    lax.fori_loop(1, chunks, pick_send, 0)

    load_hidden.wait()

    def turn(s, carry):
        at = pl.multiple_of(s * cap, cap)
        hidden_t[:, pl.ds(at, cap)] = hidden[s].T
        return carry

    lax.fori_loop(0, expert_count, turn, 0)

    def code_copy(chunk):
        return pltpu.make_async_remote_copy(
            src_ref=code.at[chunk], dst_ref=code_in.at[chunk],
            send_sem=code_send.at[chunk], recv_sem=code_recv.at[chunk],
            device_id=(mirror, me), device_id_type=MESH,
        )

    def scale_copy(chunk):
        return pltpu.make_async_remote_copy(
            src_ref=scale.at[chunk], dst_ref=scale_in.at[chunk],
            send_sem=scale_send.at[chunk], recv_sem=scale_recv.at[chunk],
            device_id=(mirror, me), device_id_type=MESH,
        )

    def store(chunk):
        start = pl.multiple_of(chunk * LANE, LANE)
        return pltpu.make_async_copy(total.at[chunk], total_hbm.at[:, pl.ds(start, LANE)], store_sem.at[chunk])

    def multiply(chunk, first, into):
        def one(i, carry):
            row = pl.multiple_of(i * tile, tile)
            rows = pl.ds(pl.multiple_of(first + row, tile), tile)
            cols = arrived[chunk].reshape(expert_count * cap, LANE)
            into[pl.ds(row, tile), :] = jnp.dot(hidden_t[rows, :], cols, preferred_element_type=jnp.float32)
            return carry

        lax.fori_loop(0, half // tile, one, 0)

    def finish(chunk):
        code_copy(chunk).wait_recv()
        scale_copy(chunk).wait_recv()
        step = scale_in[chunk, 0:1, :]
        total[chunk] = own[chunk] + code_in[chunk].astype(jnp.float32) * step
        store(chunk).start()

    def work(chunk, carry):
        all_blocks(chunk).wait_recv()
        local(chunk).wait()
        multiply(chunk, other_start, other)
        part = other[...]
        top = jnp.maximum(jnp.max(jnp.abs(part), axis=0, keepdims=True), 1e-30)
        code[chunk] = jnp.floor(part * (32766.0 / top) + 0.5).astype(jnp.int16)
        scale[chunk] = jnp.broadcast_to(top * (1.0 / 32766.0), scale.shape[1:])
        code_copy(chunk).start()
        scale_copy(chunk).start()
        multiply(chunk, own_start, own.at[chunk])

        @pl.when(chunk > 0)
        def _():
            finish(chunk - 1)

        return carry

    lax.fori_loop(0, chunks, work, 0)
    finish(chunks - 1)

    def drain(chunk, carry):
        all_blocks(chunk).wait_send()
        code_copy(chunk).wait_send()
        scale_copy(chunk).wait_send()
        store(chunk).wait()
        return carry

    lax.fori_loop(0, chunks, drain, 0)


def adamw_kernel(total_ref, master_ref, moment1_ref, moment2_ref, master_out, moment1_out, moment2_out):
    summed = total_ref[...]
    new_moment1 = 0.9 * moment1_ref[0, 0] + 0.1 * summed
    new_moment2 = 0.95 * moment2_ref[0, 0] + 0.05 * summed * summed
    master = master_ref[0, 0]
    update = new_moment1 / (1.0 - 0.9**10) / (jnp.sqrt(new_moment2 / (1.0 - 0.95**10)) + 1e-08)
    master_out[0, 0] = master - 0.2 * (update + 0.05 * master)
    moment1_out[0, 0] = new_moment1
    moment2_out[0, 0] = new_moment2


def body(out_grad, routes, saved_hidden, master, moment1, moment2):
    expert_count = lax.axis_size("expert")
    slots, width = out_grad.shape
    cap, hid = saved_hidden.shape[3:]
    half, cols = master.shape[2:]
    chunks = cols // LANE
    bf16, f32 = jnp.bfloat16, jnp.float32
    dma = pltpu.SemaphoreType.DMA
    total = pl.pallas_call(
        exchange_kernel,
        out_shape=jax.ShapeDtypeStruct((half, cols), f32),
        in_specs=[
            pl.BlockSpec(memory_space=pl.ANY),
            pl.BlockSpec(memory_space=pltpu.VMEM),
            pl.BlockSpec(memory_space=pl.ANY),
        ],
        out_specs=pl.BlockSpec(memory_space=pl.ANY),
        scratch_shapes=[
            pltpu.VMEM((slots, width), bf16),
            pltpu.VMEM((EXPG * cap, slots), bf16),
            pltpu.VMEM((chunks, expert_count, cap, LANE), bf16),
            pltpu.VMEM((chunks, expert_count, cap, LANE), bf16),
            pltpu.VMEM((expert_count, cap, hid), bf16),
            pltpu.VMEM((hid, expert_count * cap), bf16),
            pltpu.VMEM((chunks, half, LANE), f32),
            pltpu.VMEM((half, LANE), f32),
            pltpu.VMEM((chunks, half, LANE), jnp.int16),
            pltpu.VMEM((chunks, half, LANE), jnp.int16),
            pltpu.VMEM((chunks, 8, LANE), f32),
            pltpu.VMEM((chunks, 8, LANE), f32),
            pltpu.VMEM((chunks, half, LANE), f32),
            dma((2,)),
        ] + [dma((chunks,))] * 8,
        compiler_params=pltpu.CompilerParams(
            collective_id=0, has_side_effects=True, vmem_limit_bytes=56 * 1024 * 1024
        ),
        cost_estimate=pl.CostEstimate(
            flops=2 * expert_count * cap * hid * cols, bytes_accessed=16 << 20, transcendentals=0
        ),
        name="exchange",
    )(out_grad, routes.reshape(1, slots), saved_hidden)
    rows = 64
    state = pl.BlockSpec((1, 1, rows, cols), lambda i: (0, 0, i, 0))
    shape = jax.ShapeDtypeStruct((1, 1, half, cols), f32)
    return pl.pallas_call(
        adamw_kernel,
        grid=(half // rows,),
        out_shape=(shape, shape, shape),
        in_specs=[pl.BlockSpec((rows, cols), lambda i: (i, 0)), state, state, state],
        out_specs=(state, state, state),
        name="adamw",
    )(total, master, moment1, moment2)


def solution(mesh):
    in_specs = (
        P(("pipe", "expert"), None),
        P(("pipe", "expert"), None),
        P("pipe", "expert", None, None, None),
        P("pipe", "expert", None, None),
        P("pipe", "expert", None, None),
        P("pipe", "expert", None, None),
    )
    out_specs = (
        P("pipe", "expert", None, None),
        P("pipe", "expert", None, None),
        P("pipe", "expert", None, None),
    )
    return jax.shard_map(body, mesh=mesh, in_specs=in_specs, out_specs=out_specs, check_vma=False)
```

time: 222 us -> 130 us (0.59)
  the two profiles are of different devices: /device:TPU:2 before, /device:TPU:7 now
where the time goes in v1:
time: 130 us
  Pallas kernels  129 us (99%)
    pallas_call x1, Pallas kernels, body(): pl.pallas_call(exchange_kernel, out_shape=jax.ShapeDtypeStruct((half, col...  121 us
    pallas_call x1, Pallas kernels, body(): pl.pallas_call(adamw_kernel, grid=(half // rows,), out_shape=(shape, shap...  8.31 us

profile of v1, /device:TPU:7, one launch (start us, length us, event | category | flops | bytes accessed | tf_op | source)
XLA Modules:
  0.0 129.9 jit_solution(735293485010229510)
XLA Ops:
  0.6 121.0 %exchange.1.total_ref = f32[512,896]{1,0:T(8,128)} custom-call(bf16[256,7168]{1,0:T(8,128)(2,1)} %grad_hbm.1, s32[1,256]{1,0:T(1,128)} %bitcast.1, bf16[1,1,32,128,1024]{4,3,2,1,0:T(8,128)(2,1)} %hidden_hbm.1), custom_call_target="tpu_custom_call" | custom-call | flops 7516192768 | bytes 16777216 | tf_op jit(solution)/shard_map/exchange/pallas_call | solution.py:211
  121.6 8.3 %adamw.1 = (f32[1,1,512,896]{3,2,1,0:T(8,128)}, f32[1,1,512,896]{3,2,1,0:T(8,128)}, f32[1,1,512,896]{3,2,1,0:T(8,128)}) custom-call(f32[512,896]{1,0:T(8,128)} %exchange.1.total_ref, f32[1,1,512,896]{3,2,1,0:T(8,128)} %master_ref.1, f32[1,1,512,896]{3,2,1,0:T(8,128)} %moment1_ref.1, f32[1,1,512,896]{3,2,1,0:T(8,128)} %moment2_ref.1), custom_call_target="tpu_custom_call" | custom-call | tf_op jit(solution)/shard_map/adamw/pallas_call | solution.py:247

commit v2 on v1

--- a/solution.py
+++ b/solution.py
@@ -1,5 +1,3 @@
-import functools
-
 import jax
 import jax.numpy as jnp
 from jax import lax
@@ -9,13 +7,14 @@
 
 EXPG = 4
 LANE = 128
+LAG = 3
 MESH = pl.DeviceIdType.MESH
 
 
 def exchange_kernel(
-    grad_hbm, routes_ref, hidden_hbm, total_hbm,
-    grad, place, outbound, arrived, hidden, hidden_t, own, other, code, code_in, scale, scale_in, total,
-    load_sem, local_sem, send_sem, recv_sem, code_send, code_recv, scale_send, scale_recv, store_sem,
+    grad_hbm, routes_ref, hidden_hbm, master_hbm, moment1_hbm, moment2_hbm, master, moment1, moment2,
+    grad, place, outbound, arrived, hidden, hidden_t, own, other, code, code_in, scale, scale_in,
+    load_sem, local_sem, send_sem, recv_sem, code_send, code_recv, scale_send, scale_recv,
 ):
     pipe, me = lax.axis_index("pipe"), lax.axis_index("expert")
     pipe_count, expert_count = lax.axis_size("pipe"), lax.axis_size("expert")
@@ -35,6 +34,12 @@
     load_grad.start()
     load_hidden = pltpu.make_async_copy(hidden_hbm.at[0, 0], hidden, load_sem.at[1])
     load_hidden.start()
+    load_state = [
+        pltpu.make_async_copy(src.at[0, 0], dst, load_sem.at[2 + i])
+        for i, (src, dst) in enumerate(((master_hbm, master), (moment1_hbm, moment1), (moment2_hbm, moment2)))
+    ]
+    for load in load_state:
+        load.start()
 
     barrier = pltpu.get_barrier_semaphore()
 
@@ -60,17 +65,6 @@
 
     load_grad.wait()
 
-    def pick(chunk):
-        def one(j, carry):
-            start = pl.multiple_of(j * slab + chunk * LANE, LANE)
-            picked = jnp.dot(place[...], grad[:, pl.ds(start, LANE)], preferred_element_type=jnp.float32)
-            picked = picked.astype(jnp.bfloat16)
-            for k in range(EXPG):
-                outbound[chunk, k * split + j] = picked[k * cap:(k + 1) * cap]
-            return carry
-
-        lax.fori_loop(0, split, one, 0)
-
     def block(chunk, peer):
         return pltpu.make_async_remote_copy(
             src_ref=outbound.at[chunk, peer],
@@ -84,13 +78,21 @@
     def local(chunk):
         return pltpu.make_async_copy(outbound.at[chunk, me], arrived.at[chunk, me], local_sem.at[chunk])
 
-    def send(chunk):
-        def one(step, carry):
-            block(chunk, lax.rem(me + step, expert_count)).start()
-            return carry
-
-        lax.fori_loop(1, expert_count, one, 0)
-        local(chunk).start()
+    def pick_send(chunk, carry):
+        for step in range(split):
+            j = lax.rem(me + step, split)
+            start = pl.multiple_of(j * slab + chunk * LANE, LANE)
+            picked = jnp.dot(place[...], grad[:, pl.ds(start, LANE)], preferred_element_type=jnp.float32)
+            picked = picked.astype(jnp.bfloat16)
+            for k in range(EXPG):
+                outbound[chunk, k * split + j] = picked[k * cap:(k + 1) * cap]
+            for turn_k in range(EXPG):
+                k = lax.rem(me // split + EXPG - 1 - turn_k, EXPG)
+                if step == 0 and turn_k == EXPG - 1:
+                    local(chunk).start()
+                else:
+                    block(chunk, k * split + j).start()
+        return carry
 
     def all_blocks(chunk):
         others = pl.ds(0, expert_count - 1)
@@ -103,16 +105,8 @@
             device_id_type=MESH,
         )
 
-    pick(0)
     pl.semaphore_wait(barrier, expert_count)
-    send(0)
-
-    def pick_send(chunk, carry):
-        pick(chunk)
-        send(chunk)
-        return carry
-
-    lax.fori_loop(1, chunks, pick_send, 0)
+    lax.fori_loop(0, chunks, pick_send, 0)
 
     load_hidden.wait()
 
@@ -136,10 +130,6 @@
             send_sem=scale_send.at[chunk], recv_sem=scale_recv.at[chunk],
             device_id=(mirror, me), device_id_type=MESH,
         )
-
-    def store(chunk):
-        start = pl.multiple_of(chunk * LANE, LANE)
-        return pltpu.make_async_copy(total.at[chunk], total_hbm.at[:, pl.ds(start, LANE)], store_sem.at[chunk])
 
     def multiply(chunk, first, into):
         def one(i, carry):
@@ -154,9 +144,15 @@
     def finish(chunk):
         code_copy(chunk).wait_recv()
         scale_copy(chunk).wait_recv()
-        step = scale_in[chunk, 0:1, :]
-        total[chunk] = own[chunk] + code_in[chunk].astype(jnp.float32) * step
-        store(chunk).start()
+        summed = own[chunk] + code_in[chunk].astype(jnp.float32) * scale_in[chunk, 0:1, :]
+        cols = pl.ds(pl.multiple_of(chunk * LANE, LANE), LANE)
+        new_moment1 = 0.9 * moment1[:, cols] + 0.1 * summed
+        new_moment2 = 0.95 * moment2[:, cols] + 0.05 * summed * summed
+        weight = master[:, cols]
+        update = new_moment1 / (1.0 - 0.9**10) / (jnp.sqrt(new_moment2 / (1.0 - 0.95**10)) + 1e-08)
+        master[:, cols] = weight - 0.2 * (update + 0.05 * weight)
+        moment1[:, cols] = new_moment1
+        moment2[:, cols] = new_moment2
 
     def work(chunk, carry):
         all_blocks(chunk).wait_recv()
@@ -170,34 +166,29 @@
         scale_copy(chunk).start()
         multiply(chunk, own_start, own.at[chunk])
 
-        @pl.when(chunk > 0)
+        @pl.when(chunk >= LAG)
         def _():
-            finish(chunk - 1)
-
-        return carry
-
+            finish(chunk - LAG)
+
+        return carry
+
+    for load in load_state:
+        load.wait()
     lax.fori_loop(0, chunks, work, 0)
-    finish(chunks - 1)
+
+    def finish_rest(chunk, carry):
+        finish(chunk)
+        return carry
+
+    lax.fori_loop(chunks - LAG, chunks, finish_rest, 0)
 
     def drain(chunk, carry):
         all_blocks(chunk).wait_send()
         code_copy(chunk).wait_send()
         scale_copy(chunk).wait_send()
-        store(chunk).wait()
         return carry
 
     lax.fori_loop(0, chunks, drain, 0)
-
-
-def adamw_kernel(total_ref, master_ref, moment1_ref, moment2_ref, master_out, moment1_out, moment2_out):
-    summed = total_ref[...]
-    new_moment1 = 0.9 * moment1_ref[0, 0] + 0.1 * summed
-    new_moment2 = 0.95 * moment2_ref[0, 0] + 0.05 * summed * summed
-    master = master_ref[0, 0]
-    update = new_moment1 / (1.0 - 0.9**10) / (jnp.sqrt(new_moment2 / (1.0 - 0.95**10)) + 1e-08)
-    master_out[0, 0] = master - 0.2 * (update + 0.05 * master)
-    moment1_out[0, 0] = new_moment1
-    moment2_out[0, 0] = new_moment2
 
 
 def body(out_grad, routes, saved_hidden, master, moment1, moment2):
@@ -208,15 +199,19 @@
     chunks = cols // LANE
     bf16, f32 = jnp.bfloat16, jnp.float32
     dma = pltpu.SemaphoreType.DMA
-    total = pl.pallas_call(
+    state = pltpu.VMEM((half, cols), f32)
+    states = pl.pallas_call(
         exchange_kernel,
-        out_shape=jax.ShapeDtypeStruct((half, cols), f32),
+        out_shape=(state, state, state),
         in_specs=[
             pl.BlockSpec(memory_space=pl.ANY),
             pl.BlockSpec(memory_space=pltpu.VMEM),
             pl.BlockSpec(memory_space=pl.ANY),
+            pl.BlockSpec(memory_space=pl.ANY),
+            pl.BlockSpec(memory_space=pl.ANY),
+            pl.BlockSpec(memory_space=pl.ANY),
         ],
-        out_specs=pl.BlockSpec(memory_space=pl.ANY),
+        out_specs=[pl.BlockSpec(memory_space=pltpu.VMEM)] * 3,
         scratch_shapes=[
             pltpu.VMEM((slots, width), bf16),
             pltpu.VMEM((EXPG * cap, slots), bf16),
@@ -230,28 +225,17 @@
             pltpu.VMEM((chunks, half, LANE), jnp.int16),
             pltpu.VMEM((chunks, 8, LANE), f32),
             pltpu.VMEM((chunks, 8, LANE), f32),
-            pltpu.VMEM((chunks, half, LANE), f32),
-            dma((2,)),
-        ] + [dma((chunks,))] * 8,
+            dma((5,)),
+        ] + [dma((chunks,))] * 7,
         compiler_params=pltpu.CompilerParams(
-            collective_id=0, has_side_effects=True, vmem_limit_bytes=56 * 1024 * 1024
+            collective_id=0, has_side_effects=True, vmem_limit_bytes=48 * 1024 * 1024
         ),
         cost_estimate=pl.CostEstimate(
             flops=2 * expert_count * cap * hid * cols, bytes_accessed=16 << 20, transcendentals=0
         ),
         name="exchange",
-    )(out_grad, routes.reshape(1, slots), saved_hidden)
-    rows = 64
-    state = pl.BlockSpec((1, 1, rows, cols), lambda i: (0, 0, i, 0))
-    shape = jax.ShapeDtypeStruct((1, 1, half, cols), f32)
-    return pl.pallas_call(
-        adamw_kernel,
-        grid=(half // rows,),
-        out_shape=(shape, shape, shape),
-        in_specs=[pl.BlockSpec((rows, cols), lambda i: (i, 0)), state, state, state],
-        out_specs=(state, state, state),
-        name="adamw",
-    )(total, master, moment1, moment2)
+    )(out_grad, routes.reshape(1, slots), saved_hidden, master, moment1, moment2)
+    return tuple(new.reshape(1, 1, half, cols) for new in states)
 
 
 def solution(mesh):

time: 130 us -> 118 us (0.908)
  the two profiles are of different devices: /device:TPU:7 before, /device:TPU:1 now
where the time goes in v2:
time: 118 us
  Pallas kernels  113 us (96%)
  local copies, waits for them, and re-layouts  4.36 us (4%)
    pallas_call x1, Pallas kernels, body(): pl.pallas_call(exchange_kernel, out_shape=(state, state, state), in_specs...  113 us
    unnamed x5, local copies, waits for them, and re-layouts  4.36 us

profile of v2, /device:TPU:1, one launch (start us, length us, event | category | flops | bytes accessed | tf_op | source)
XLA Modules:
  0.0 118.0 jit_solution(3001137318072521835)
XLA Ops:
  0.6 0.0 copy-start
  0.6 0.7 copy-done
  1.3 113.0 %exchange.1 = (f32[512,896]{1,0:T(8,128)S(1)}, f32[512,896]{1,0:T(8,128)S(1)}, f32[512,896]{1,0:T(8,128)S(1)}) custom-call(bf16[256,7168]{1,0:T(8,128)(2,1)} %grad_hbm.1, s32[1,256]{1,0:T(1,128)S(1)} %bitcast.7, bf16[1,1,32,128,1024]{4,3,2,1,0:T(8,128)(2,1)} %hidden_hbm.1, f32[1,1,512,896]{3,2,1,0:T(8,128)} %master_hbm.1, f32[1,1,512,896]{3,2,1,0:T(8,128)} %moment1_hbm.1, ...), custom_call_target="tpu_custom_call" | custom-call | flops 7516192768 | bytes 16777216 | tf_op jit(solution)/shard_map/exchange/pallas_call | solution.py:203
  114.3 1.2 %copy.12 = f32[1,1,512,896]{3,2,1,0:T(8,128)} copy(f32[1,1,512,896]{3,2,1,0:T(8,128)S(1)} %bitcast.6) | data formatting | bytes 3670016
  115.5 1.2 %copy.13 = f32[1,1,512,896]{3,2,1,0:T(8,128)} copy(f32[1,1,512,896]{3,2,1,0:T(8,128)S(1)} %bitcast.5) | data formatting | bytes 3670016
  116.8 1.2 %copy.14 = f32[1,1,512,896]{3,2,1,0:T(8,128)} copy(f32[1,1,512,896]{3,2,1,0:T(8,128)S(1)} %bitcast.4) | data formatting | bytes 3670016
Async XLA Ops:
  0.6 0.7 copy-start

commit v3 on v2

--- a/solution.py
+++ b/solution.py
@@ -12,8 +12,8 @@
 
 
 def exchange_kernel(
-    grad_hbm, routes_ref, hidden_hbm, master_hbm, moment1_hbm, moment2_hbm, master, moment1, moment2,
-    grad, place, outbound, arrived, hidden, hidden_t, own, other, code, code_in, scale, scale_in,
+    grad_hbm, routes_hbm, hidden_hbm, master_hbm, moment1_hbm, moment2_hbm, master, moment1, moment2,
+    grad, routes, place, outbound, arrived, hidden, hidden_t, own, other, code, code_in, scale, scale_in,
     load_sem, local_sem, send_sem, recv_sem, code_send, code_recv, scale_send, scale_recv,
 ):
     pipe, me = lax.axis_index("pipe"), lax.axis_index("expert")
@@ -32,6 +32,8 @@
 
     load_grad = pltpu.make_async_copy(grad_hbm, grad, load_sem.at[0])
     load_grad.start()
+    load_routes = pltpu.make_async_copy(routes_hbm, routes, load_sem.at[5])
+    load_routes.start()
     load_hidden = pltpu.make_async_copy(hidden_hbm.at[0, 0], hidden, load_sem.at[1])
     load_hidden.start()
     load_state = [
@@ -52,7 +54,8 @@
     lax.fori_loop(1, expert_count, greet, 0)
     pl.semaphore_signal(barrier, inc=1, device_id=(mirror, me), device_id_type=MESH)
 
-    route = routes_ref[...]
+    load_routes.wait()
+    route = routes[...]
     chosen = jnp.broadcast_to(route, (8, slots)) == lax.broadcasted_iota(jnp.int32, (8, slots), 0)
     earlier = lax.broadcasted_iota(jnp.int32, (slots, slots), 0) < lax.broadcasted_iota(jnp.int32, (slots, slots), 1)
     before = jnp.dot(
@@ -191,6 +194,18 @@
     lax.fori_loop(0, chunks, drain, 0)
 
 
+def store_kernel(*refs):
+    count = len(refs) // 2
+    sems = refs[-1]
+    copies = [
+        pltpu.make_async_copy(refs[i], refs[count + i].at[0, 0], sems.at[i]) for i in range(count)
+    ]
+    for copy in copies:
+        copy.start()
+    for copy in copies:
+        copy.wait()
+
+
 def body(out_grad, routes, saved_hidden, master, moment1, moment2):
     expert_count = lax.axis_size("expert")
     slots, width = out_grad.shape
@@ -205,7 +220,7 @@
         out_shape=(state, state, state),
         in_specs=[
             pl.BlockSpec(memory_space=pl.ANY),
-            pl.BlockSpec(memory_space=pltpu.VMEM),
+            pl.BlockSpec(memory_space=pltpu.HBM),
             pl.BlockSpec(memory_space=pl.ANY),
             pl.BlockSpec(memory_space=pl.ANY),
             pl.BlockSpec(memory_space=pl.ANY),
@@ -214,6 +229,7 @@
         out_specs=[pl.BlockSpec(memory_space=pltpu.VMEM)] * 3,
         scratch_shapes=[
             pltpu.VMEM((slots, width), bf16),
+            pltpu.VMEM((1, slots), jnp.int32),
             pltpu.VMEM((EXPG * cap, slots), bf16),
             pltpu.VMEM((chunks, expert_count, cap, LANE), bf16),
             pltpu.VMEM((chunks, expert_count, cap, LANE), bf16),
@@ -225,7 +241,7 @@
             pltpu.VMEM((chunks, half, LANE), jnp.int16),
             pltpu.VMEM((chunks, 8, LANE), f32),
             pltpu.VMEM((chunks, 8, LANE), f32),
-            dma((5,)),
+            dma((6,)),
         ] + [dma((chunks,))] * 7,
         compiler_params=pltpu.CompilerParams(
             collective_id=0, has_side_effects=True, vmem_limit_bytes=48 * 1024 * 1024
@@ -234,8 +250,17 @@
             flops=2 * expert_count * cap * hid * cols, bytes_accessed=16 << 20, transcendentals=0
         ),
         name="exchange",
-    )(out_grad, routes.reshape(1, slots), saved_hidden, master, moment1, moment2)
-    return tuple(new.reshape(1, 1, half, cols) for new in states)
+    )(out_grad, pltpu.with_memory_space_constraint(routes.reshape(1, slots), pltpu.HBM), saved_hidden, master, moment1, moment2)
+    shape = jax.ShapeDtypeStruct((1, 1, half, cols), f32)
+    return pl.pallas_call(
+        store_kernel,
+        out_shape=(shape, shape, shape),
+        in_specs=[pl.BlockSpec(memory_space=pltpu.VMEM)] * 3,
+        out_specs=[pl.BlockSpec(memory_space=pl.ANY)] * 3,
+        scratch_shapes=[dma((3,))],
+        compiler_params=pltpu.CompilerParams(vmem_limit_bytes=1024 * 1024),
+        name="store",
+    )(*(pltpu.with_memory_space_constraint(new, pltpu.VMEM) for new in states))
 
 
 def solution(mesh):

time: 118 us -> 116 us (0.983)
  local copies, waits for them, and re-layouts: 4.36 us -> 0 us
  Pallas kernels: 113 us -> 116 us
    unnamed x5 -> x0, local copies, waits for them, and re-layouts: 4.36 us -> none
    pallas_call x0 -> x1, Pallas kernels: none -> 2.46 us  [body(): pl.pallas_call(store_kernel, out_shape=(shape, shape, shape), in_specs=[p...]
where the time goes in v3:
time: 116 us
  Pallas kernels  116 us (100%)
    pallas_call x1, Pallas kernels, body(): pl.pallas_call(exchange_kernel, out_shape=(state, state, state), in_specs...  113 us
    pallas_call x1, Pallas kernels, body(): pl.pallas_call(store_kernel, out_shape=(shape, shape, shape), in_specs=[p...  2.46 us

profile of v3, /device:TPU:1, one launch (start us, length us, event | category | flops | bytes accessed | tf_op | source)
XLA Modules:
  0.0 116.3 jit_solution(3025028234024381394)
XLA Ops:
  0.6 113.2 %exchange.1 = (f32[512,896]{1,0:T(8,128)S(1)}, f32[512,896]{1,0:T(8,128)S(1)}, f32[512,896]{1,0:T(8,128)S(1)}) custom-call(bf16[256,7168]{1,0:T(8,128)(2,1)} %grad_hbm.1, s32[1,256]{1,0:T(1,128)} %bitcast.1, bf16[1,1,32,128,1024]{4,3,2,1,0:T(8,128)(2,1)} %hidden_hbm.1, f32[1,1,512,896]{3,2,1,0:T(8,128)} %master_hbm.1, f32[1,1,512,896]{3,2,1,0:T(8,128)} %moment1_hbm.1, ...), custom_call_target="tpu_custom_call" | custom-call | flops 7516192768 | bytes 16777216 | tf_op jit(solution)/shard_map/exchange/pallas_call | solution.py:218
  113.9 2.5 %store.1 = (f32[1,1,512,896]{3,2,1,0:T(8,128)}, f32[1,1,512,896]{3,2,1,0:T(8,128)}, f32[1,1,512,896]{3,2,1,0:T(8,128)}) custom-call(f32[512,896]{1,0:T(8,128)S(1)} %get-tuple-element.6.refs_0_, f32[512,896]{1,0:T(8,128)S(1)} %get-tuple-element.7.refs_1_, f32[512,896]{1,0:T(8,128)S(1)} %get-tuple-element.8.refs_2_), custom_call_target="tpu_custom_call" | custom-call | tf_op jit(solution)/shard_map/store/pallas_call | solution.py:255

commit v4 on v3

--- a/solution.py
+++ b/solution.py
@@ -8,6 +8,8 @@
 EXPG = 4
 LANE = 128
 LAG = 3
+AHEAD = 3
+CROSSING = 208
 MESH = pl.DeviceIdType.MESH
 
 
@@ -194,6 +196,337 @@
     lax.fori_loop(0, chunks, drain, 0)
 
 
+def relay_kernel(
+    grad_hbm, routes_hbm, hidden_hbm, master_hbm, moment1_hbm, moment2_hbm, master, moment1, moment2, over_out,
+    grad, routes, routes_in, place, pack, expand, packed, packed_in, outbound, arrived, hidden, hidden_t,
+    own, other, code, code_in, scale, scale_in, over_plane, over_pair, over_pipe,
+    load_sem, hidden_sem, routes_sem, over_sem, pack_send, pack_recv, local_sem, send_sem, recv_sem,
+    code_send, code_recv, scale_send, scale_recv,
+):
+    pipe, me = lax.axis_index("pipe"), lax.axis_index("expert")
+    pipe_count, expert_count = lax.axis_size("pipe"), lax.axis_size("expert")
+    chunks, _, plane, cap, _ = outbound.shape
+    slots, width = grad.shape
+    split = expert_count // EXPG
+    slab = width // split
+    hid = hidden_t.shape[0]
+    half = hid // 2
+    mirror = pipe_count - 1 - pipe
+    keep_high = pipe // (pipe_count // 2)
+    own_start = pl.multiple_of(keep_high * half, half)
+    other_start = pl.multiple_of((1 - keep_high) * half, half)
+    tile = half // 2
+    side = me // plane
+    seat = me % plane
+    base = side * plane
+    partner = lax.rem(me + plane, expert_count)
+    local_experts = EXPG // 2
+    bound = packed.shape[2]
+
+    load_routes = pltpu.make_async_copy(routes_hbm, routes, load_sem.at[0])
+    load_routes.start()
+    load_grad = pltpu.make_async_copy(grad_hbm, grad, load_sem.at[1])
+    load_grad.start()
+    group = hidden.shape[1]
+
+    def load_hidden(turn):
+        return pltpu.make_async_copy(
+            hidden_hbm.at[0, 0, pl.ds(turn * group, group)], hidden.at[turn % 2], hidden_sem.at[turn % 2]
+        )
+
+    load_hidden(0).start()
+    load_hidden(1).start()
+    load_state = [
+        pltpu.make_async_copy(src.at[0, 0], dst, load_sem.at[2 + i])
+        for i, (src, dst) in enumerate(((master_hbm, master), (moment1_hbm, moment1), (moment2_hbm, moment2)))
+    ]
+    for load in load_state:
+        load.start()
+
+    barrier = pltpu.get_barrier_semaphore()
+
+    def greet(step, carry):
+        pl.semaphore_signal(
+            barrier, inc=1, device_id=(pipe, base + lax.rem(seat + step, plane)), device_id_type=MESH
+        )
+        return carry
+
+    lax.fori_loop(1, plane, greet, 0)
+    pl.semaphore_signal(barrier, inc=1, device_id=(pipe, partner), device_id_type=MESH)
+    for step in range(1, pipe_count):
+        pl.semaphore_signal(barrier, inc=1, device_id=(lax.rem(pipe + step, pipe_count), me), device_id_type=MESH)
+
+    def one_hots(route, packed_side):
+        expert = lax.broadcasted_iota(jnp.int32, (8, slots), 0)
+        chosen = jnp.broadcast_to(route, (8, slots)) == expert
+        earlier = lax.broadcasted_iota(jnp.int32, (slots, slots), 0) < lax.broadcasted_iota(jnp.int32, (slots, slots), 1)
+        before = jnp.dot(
+            chosen.astype(jnp.bfloat16), earlier.astype(jnp.bfloat16), preferred_element_type=jnp.float32
+        )
+        rank = jnp.sum(jnp.where(chosen, before, 0.0), axis=0, keepdims=True).astype(jnp.int32)
+        flat = jnp.broadcast_to((route - side * local_experts) * cap + rank, (local_experts * cap, slots))
+        places = flat == lax.broadcasted_iota(jnp.int32, (local_experts * cap, slots), 0)
+        first = packed_side * local_experts
+        in_side = (expert >= first) & (expert < first + local_experts)
+        order = jnp.sum(jnp.where(in_side, before, 0.0), axis=0, keepdims=True).astype(jnp.int32)
+        goes = (route >= first) & (route < first + local_experts)
+        order = jnp.broadcast_to(jnp.where(goes, order, -1), (bound, slots))
+        ranks = order == lax.broadcasted_iota(jnp.int32, (bound, slots), 0)
+        return places.astype(jnp.bfloat16), ranks.astype(jnp.bfloat16), goes
+
+    load_routes.wait()
+    own_places, own_ranks, goes = one_hots(routes[...], 1 - side)
+    place[...] = own_places
+    pack[...] = own_ranks
+    crossing = jnp.sum(goes.astype(jnp.float32), axis=1, keepdims=True)
+    over = jnp.broadcast_to((crossing > bound).astype(jnp.int32), over_pair.shape[1:])
+    over_plane[seat] = over
+
+    load_grad.wait()
+    pl.semaphore_wait(barrier, plane - 1 + 1 + pipe_count - 1)
+
+    send_routes = pltpu.make_async_remote_copy(
+        src_ref=routes, dst_ref=routes_in, send_sem=routes_sem.at[0], recv_sem=routes_sem.at[1],
+        device_id=(pipe, partner), device_id_type=MESH,
+    )
+    send_routes.start()
+
+    def over_to_plane(seat_to):
+        return pltpu.make_async_remote_copy(
+            src_ref=over_plane.at[seat], dst_ref=over_plane.at[seat],
+            send_sem=over_sem.at[0], recv_sem=over_sem.at[1],
+            device_id=(pipe, base + seat_to), device_id_type=MESH,
+        )
+
+    def tell_plane(step, carry):
+        over_to_plane(lax.rem(seat + step, plane)).start()
+        return carry
+
+    over_all_plane = pltpu.make_async_remote_copy(
+        src_ref=over_plane.at[pl.ds(0, plane - 1)], dst_ref=over_plane.at[pl.ds(0, plane - 1)],
+        send_sem=over_sem.at[0], recv_sem=over_sem.at[1],
+        device_id=(pipe, partner), device_id_type=MESH,
+    )
+    over_to_partner = pltpu.make_async_remote_copy(
+        src_ref=over_pair.at[0], dst_ref=over_pair.at[1],
+        send_sem=over_sem.at[2], recv_sem=over_sem.at[3],
+        device_id=(pipe, partner), device_id_type=MESH,
+    )
+    over_to_pipes = [
+        pltpu.make_async_remote_copy(
+            src_ref=over_pipe.at[pipe], dst_ref=over_pipe.at[pipe],
+            send_sem=over_sem.at[4], recv_sem=over_sem.at[5],
+            device_id=(lax.rem(pipe + step, pipe_count), me), device_id_type=MESH,
+        )
+        for step in range(1, pipe_count)
+    ]
+    over_all_pipes = pltpu.make_async_remote_copy(
+        src_ref=over_pipe.at[pl.ds(0, pipe_count - 1)], dst_ref=over_pipe.at[pl.ds(0, pipe_count - 1)],
+        send_sem=over_sem.at[4], recv_sem=over_sem.at[5],
+        device_id=(mirror, me), device_id_type=MESH,
+    )
+
+    def block(chunk, kind, to):
+        return pltpu.make_async_remote_copy(
+            src_ref=outbound.at[chunk, kind, to],
+            dst_ref=arrived.at[chunk, me if kind == 0 else partner],
+            send_sem=send_sem.at[kind, chunk],
+            recv_sem=recv_sem.at[kind, chunk],
+            device_id=(pipe, base + to),
+            device_id_type=MESH,
+        )
+
+    def local(chunk, kind):
+        return pltpu.make_async_copy(
+            outbound.at[chunk, kind, seat],
+            arrived.at[chunk, me if kind == 0 else partner],
+            local_sem.at[kind, chunk],
+        )
+
+    def all_blocks(chunk, kind):
+        others = pl.ds(0, plane - 1)
+        return pltpu.make_async_remote_copy(
+            src_ref=outbound.at[chunk, kind, others],
+            dst_ref=arrived.at[chunk, others],
+            send_sem=send_sem.at[kind, chunk],
+            recv_sem=recv_sem.at[kind, chunk],
+            device_id=(pipe, partner),
+            device_id_type=MESH,
+        )
+
+    def spread(chunk, kind, step, j, rows):
+        rows = rows.astype(jnp.bfloat16)
+        for k in range(local_experts):
+            outbound[chunk, kind, k * split + j] = rows[k * cap:(k + 1) * cap]
+        for turn in range(local_experts):
+            k = lax.rem(seat // split + local_experts - 1 - turn, local_experts)
+            if step == 0 and turn == local_experts - 1:
+                local(chunk, kind).start()
+            else:
+                block(chunk, kind, k * split + j).start()
+
+    def slab_cols(chunk, j):
+        return pl.ds(pl.multiple_of(j * slab + chunk * LANE, LANE), LANE)
+
+    def send_own(chunk):
+        for step in range(split):
+            j = lax.rem(seat + step, split)
+            rows = jnp.dot(place[...], grad[:, slab_cols(chunk, j)], preferred_element_type=jnp.float32)
+            spread(chunk, 0, step, j, rows)
+
+    def packed_copy(chunk):
+        return pltpu.make_async_remote_copy(
+            src_ref=packed.at[chunk], dst_ref=packed_in.at[chunk],
+            send_sem=pack_send.at[chunk], recv_sem=pack_recv.at[chunk],
+            device_id=(pipe, partner), device_id_type=MESH,
+        )
+
+    def send_packed(chunk):
+        for j in range(split):
+            rows = jnp.dot(pack[...], grad[:, slab_cols(chunk, j)], preferred_element_type=jnp.float32)
+            packed[chunk, j] = rows.astype(jnp.bfloat16)
+        packed_copy(chunk).start()
+
+    def first_sends(chunk, carry):
+        send_own(chunk)
+        send_packed(chunk)
+        return carry
+
+    first_sends(0, 0)
+    lax.fori_loop(1, plane, tell_plane, 0)
+    lax.fori_loop(1, chunks, first_sends, 0)
+
+    send_routes.wait_recv()
+    their_places, their_ranks, _ = one_hots(routes_in[...], side)
+    expand[...] = lax.dot_general(
+        their_places, their_ranks, (((1,), (1,)), ((), ())), preferred_element_type=jnp.float32
+    ).astype(jnp.bfloat16)
+
+    def relay(chunk):
+        packed_copy(chunk).wait_recv()
+        for step in range(split):
+            j = lax.rem(seat + step, split)
+            rows = jnp.dot(expand[...], packed_in[chunk, j], preferred_element_type=jnp.float32)
+            spread(chunk, 1, step, j, rows)
+
+    relay(0)
+
+    turns = expert_count // group
+    for turn in range(turns):
+        load_hidden(turn).wait()
+
+        def flip(i, carry):
+            at = pl.multiple_of((turn * group + i) * cap, cap)
+            hidden_t[:, pl.ds(at, cap)] = hidden[turn % 2, i].T
+            return carry
+
+        lax.fori_loop(0, group, flip, 0)
+        if turn + 2 < turns:
+            load_hidden(turn + 2).start()
+
+    over_all_plane.wait_recv()
+    over_pair[0] = jnp.max(over_plane[...], axis=0)
+    over_to_partner.start()
+
+    def relay_one(chunk, carry):
+        relay(chunk)
+        return carry
+
+    lax.fori_loop(1, AHEAD, relay_one, 0)
+
+    over_to_partner.wait_recv()
+    over_pipe[pipe] = jnp.maximum(over_pair[0], over_pair[1])
+    for copy in over_to_pipes:
+        copy.start()
+
+    def code_copy(chunk):
+        return pltpu.make_async_remote_copy(
+            src_ref=code.at[chunk], dst_ref=code_in.at[chunk],
+            send_sem=code_send.at[chunk], recv_sem=code_recv.at[chunk],
+            device_id=(mirror, me), device_id_type=MESH,
+        )
+
+    def scale_copy(chunk):
+        return pltpu.make_async_remote_copy(
+            src_ref=scale.at[chunk], dst_ref=scale_in.at[chunk],
+            send_sem=scale_send.at[chunk], recv_sem=scale_recv.at[chunk],
+            device_id=(mirror, me), device_id_type=MESH,
+        )
+
+    def multiply(chunk, first, into):
+        def one(i, carry):
+            row = pl.multiple_of(i * tile, tile)
+            rows = pl.ds(pl.multiple_of(first + row, tile), tile)
+            cols = arrived[chunk].reshape(expert_count * cap, LANE)
+            into[pl.ds(row, tile), :] = jnp.dot(hidden_t[rows, :], cols, preferred_element_type=jnp.float32)
+            return carry
+
+        lax.fori_loop(0, half // tile, one, 0)
+
+    def finish(chunk):
+        code_copy(chunk).wait_recv()
+        scale_copy(chunk).wait_recv()
+        summed = own[chunk] + code_in[chunk].astype(jnp.float32) * scale_in[chunk, 0:1, :]
+        cols = pl.ds(pl.multiple_of(chunk * LANE, LANE), LANE)
+        new_moment1 = 0.9 * moment1[:, cols] + 0.1 * summed
+        new_moment2 = 0.95 * moment2[:, cols] + 0.05 * summed * summed
+        weight = master[:, cols]
+        update = new_moment1 / (1.0 - 0.9**10) / (jnp.sqrt(new_moment2 / (1.0 - 0.95**10)) + 1e-08)
+        master[:, cols] = weight - 0.2 * (update + 0.05 * weight)
+        moment1[:, cols] = new_moment1
+        moment2[:, cols] = new_moment2
+
+    def work(chunk, carry):
+        @pl.when(chunk + AHEAD < chunks)
+        def _():
+            relay(chunk + AHEAD)
+
+        for kind in range(2):
+            all_blocks(chunk, kind).wait_recv()
+            local(chunk, kind).wait()
+        multiply(chunk, other_start, other)
+        part = other[...]
+        top = jnp.maximum(jnp.max(jnp.abs(part), axis=0, keepdims=True), 1e-30)
+        code[chunk] = jnp.floor(part * (32766.0 / top) + 0.5).astype(jnp.int16)
+        scale[chunk] = jnp.broadcast_to(top * (1.0 / 32766.0), scale.shape[1:])
+        code_copy(chunk).start()
+        scale_copy(chunk).start()
+        multiply(chunk, own_start, own.at[chunk])
+
+        @pl.when(chunk >= LAG)
+        def _():
+            finish(chunk - LAG)
+
+        return carry
+
+    for load in load_state:
+        load.wait()
+    lax.fori_loop(0, chunks, work, 0)
+
+    def finish_rest(chunk, carry):
+        finish(chunk)
+        return carry
+
+    lax.fori_loop(chunks - LAG, chunks, finish_rest, 0)
+
+    over_all_pipes.wait_recv()
+    over_out[...] = jnp.max(over_pipe[...], axis=0)
+    send_routes.wait_send()
+    over_all_plane.wait_send()
+    over_to_partner.wait_send()
+    over_all_pipes.wait_send()
+
+    def drain(chunk, carry):
+        for kind in range(2):
+            all_blocks(chunk, kind).wait_send()
+        packed_copy(chunk).wait_send()
+        code_copy(chunk).wait_send()
+        scale_copy(chunk).wait_send()
+        return carry
+
+    lax.fori_loop(0, chunks, drain, 0)
+
+
 def store_kernel(*refs):
     count = len(refs) // 2
     sems = refs[-1]
@@ -214,26 +547,82 @@
     chunks = cols // LANE
     bf16, f32 = jnp.bfloat16, jnp.float32
     dma = pltpu.SemaphoreType.DMA
+    split, plane = expert_count // EXPG, expert_count // 2
     state = pltpu.VMEM((half, cols), f32)
-    states = pl.pallas_call(
-        exchange_kernel,
-        out_shape=(state, state, state),
-        in_specs=[
-            pl.BlockSpec(memory_space=pl.ANY),
-            pl.BlockSpec(memory_space=pltpu.HBM),
-            pl.BlockSpec(memory_space=pl.ANY),
-            pl.BlockSpec(memory_space=pl.ANY),
-            pl.BlockSpec(memory_space=pl.ANY),
-            pl.BlockSpec(memory_space=pl.ANY),
-        ],
-        out_specs=[pl.BlockSpec(memory_space=pltpu.VMEM)] * 3,
+    operands = (
+        out_grad, pltpu.with_memory_space_constraint(routes.reshape(1, slots), pltpu.HBM), saved_hidden,
+        master, moment1, moment2,
+    )
+
+    def every_row():
+        states = pl.pallas_call(
+            exchange_kernel,
+            out_shape=(state, state, state),
+            in_specs=[
+                pl.BlockSpec(memory_space=pl.ANY),
+                pl.BlockSpec(memory_space=pltpu.HBM),
+                pl.BlockSpec(memory_space=pl.ANY),
+                pl.BlockSpec(memory_space=pl.ANY),
+                pl.BlockSpec(memory_space=pl.ANY),
+                pl.BlockSpec(memory_space=pl.ANY),
+            ],
+            out_specs=[pl.BlockSpec(memory_space=pltpu.VMEM)] * 3,
+            scratch_shapes=[
+                pltpu.VMEM((slots, width), bf16),
+                pltpu.VMEM((1, slots), jnp.int32),
+                pltpu.VMEM((EXPG * cap, slots), bf16),
+                pltpu.VMEM((chunks, expert_count, cap, LANE), bf16),
+                pltpu.VMEM((chunks, expert_count, cap, LANE), bf16),
+                pltpu.VMEM((expert_count, cap, hid), bf16),
+                pltpu.VMEM((hid, expert_count * cap), bf16),
+                pltpu.VMEM((chunks, half, LANE), f32),
+                pltpu.VMEM((half, LANE), f32),
+                pltpu.VMEM((chunks, half, LANE), jnp.int16),
+                pltpu.VMEM((chunks, half, LANE), jnp.int16),
+                pltpu.VMEM((chunks, 8, LANE), f32),
+                pltpu.VMEM((chunks, 8, LANE), f32),
+                dma((6,)),
+            ] + [dma((chunks,))] * 7,
+            compiler_params=pltpu.CompilerParams(
+                collective_id=1, has_side_effects=True, vmem_limit_bytes=48 * 1024 * 1024
+            ),
+            cost_estimate=pl.CostEstimate(
+                flops=2 * expert_count * cap * hid * cols, bytes_accessed=16 << 20, transcendentals=0
+            ),
+            name="exchange",
+        )(*operands)
+        return stored(states)
+
+    def stored(states):
+        shape = jax.ShapeDtypeStruct((1, 1, half, cols), f32)
+        return pl.pallas_call(
+            store_kernel,
+            out_shape=(shape, shape, shape),
+            in_specs=[pl.BlockSpec(memory_space=pltpu.VMEM)] * 3,
+            out_specs=[pl.BlockSpec(memory_space=pl.ANY)] * 3,
+            scratch_shapes=[dma((3,))],
+            compiler_params=pltpu.CompilerParams(vmem_limit_bytes=1024 * 1024),
+            name="store",
+        )(*(pltpu.with_memory_space_constraint(new, pltpu.VMEM) for new in states))
+
+    *states, over = pl.pallas_call(
+        relay_kernel,
+        out_shape=(state, state, state, jax.ShapeDtypeStruct((8, LANE), jnp.int32)),
+        in_specs=[pl.BlockSpec(memory_space=pl.ANY), pl.BlockSpec(memory_space=pltpu.HBM)]
+        + [pl.BlockSpec(memory_space=pl.ANY)] * 4,
+        out_specs=[pl.BlockSpec(memory_space=pltpu.VMEM)] * 4,
         scratch_shapes=[
             pltpu.VMEM((slots, width), bf16),
             pltpu.VMEM((1, slots), jnp.int32),
-            pltpu.VMEM((EXPG * cap, slots), bf16),
+            pltpu.VMEM((1, slots), jnp.int32),
+            pltpu.VMEM((EXPG // 2 * cap, slots), bf16),
+            pltpu.VMEM((CROSSING, slots), bf16),
+            pltpu.VMEM((EXPG // 2 * cap, CROSSING), bf16),
+            pltpu.VMEM((chunks, split, CROSSING, LANE), bf16),
+            pltpu.VMEM((chunks, split, CROSSING, LANE), bf16),
+            pltpu.VMEM((chunks, 2, plane, cap, LANE), bf16),
             pltpu.VMEM((chunks, expert_count, cap, LANE), bf16),
-            pltpu.VMEM((chunks, expert_count, cap, LANE), bf16),
-            pltpu.VMEM((expert_count, cap, hid), bf16),
+            pltpu.VMEM((2, expert_count // 8, cap, hid), bf16),
             pltpu.VMEM((hid, expert_count * cap), bf16),
             pltpu.VMEM((chunks, half, LANE), f32),
             pltpu.VMEM((half, LANE), f32),
@@ -241,26 +630,29 @@
             pltpu.VMEM((chunks, half, LANE), jnp.int16),
             pltpu.VMEM((chunks, 8, LANE), f32),
             pltpu.VMEM((chunks, 8, LANE), f32),
+            pltpu.VMEM((plane, 8, LANE), jnp.int32),
+            pltpu.VMEM((2, 8, LANE), jnp.int32),
+            pltpu.VMEM((lax.axis_size("pipe"), 8, LANE), jnp.int32),
+            dma((5,)),
+            dma((2,)),
+            dma((2,)),
             dma((6,)),
-        ] + [dma((chunks,))] * 7,
+            dma((chunks,)),
+            dma((chunks,)),
+            dma((2, chunks)),
+            dma((2, chunks)),
+            dma((2, chunks)),
+        ] + [dma((chunks,))] * 4,
         compiler_params=pltpu.CompilerParams(
             collective_id=0, has_side_effects=True, vmem_limit_bytes=48 * 1024 * 1024
         ),
         cost_estimate=pl.CostEstimate(
             flops=2 * expert_count * cap * hid * cols, bytes_accessed=16 << 20, transcendentals=0
         ),
-        name="exchange",
-    )(out_grad, pltpu.with_memory_space_constraint(routes.reshape(1, slots), pltpu.HBM), saved_hidden, master, moment1, moment2)
-    shape = jax.ShapeDtypeStruct((1, 1, half, cols), f32)
-    return pl.pallas_call(
-        store_kernel,
-        out_shape=(shape, shape, shape),
-        in_specs=[pl.BlockSpec(memory_space=pltpu.VMEM)] * 3,
-        out_specs=[pl.BlockSpec(memory_space=pl.ANY)] * 3,
-        scratch_shapes=[dma((3,))],
-        compiler_params=pltpu.CompilerParams(vmem_limit_bytes=1024 * 1024),
-        name="store",
-    )(*(pltpu.with_memory_space_constraint(new, pltpu.VMEM) for new in states))
+        name="relay",
+    )(*operands)
+    done = stored(states)
+    return lax.cond(over[0, 0] > 0, every_row, lambda: done)
 
 
 def solution(mesh):

time: 116 us -> 115 us (level)
  Pallas kernels: 116 us -> 113 us
    pallas_call x2, Pallas kernels: 116 us -> 113 us  [the longest x1 110 us: body(): pl.pallas_call(relay_kernel, out_shape=(state, state, state, jax.ShapeDty...]
where the time goes in v4:
time: 115 us; the launch traced here: 114 us
  Pallas kernels  113 us (98%)
  between operations  1.32 us (1%)
    pallas_call x1, Pallas kernels, body(): pl.pallas_call(relay_kernel, out_shape=(state, state, state, jax.ShapeDty...  110 us
    pallas_call x1, Pallas kernels, stored(): pl.pallas_call(store_kernel, out_shape=(shape, shape, shape), in_specs=[p...  2.46 us

profile of v4, /device:TPU:1, one launch (start us, length us, event | category | flops | bytes accessed | tf_op | source)
XLA Modules:
  0.0 114.4 jit_solution(8584111734015638862)
XLA Ops:
  0.6 0.0 copy-start
  0.6 110.1 %relay.1 = (f32[512,896]{1,0:T(8,128)S(1)}, f32[512,896]{1,0:T(8,128)S(1)}, f32[512,896]{1,0:T(8,128)S(1)}, s32[8,128]{1,0:T(8,128)S(1)}) custom-call(bf16[256,7168]{1,0:T(8,128)(2,1)} %grad_hbm.1, s32[1,256]{1,0:T(1,128)} %bitcast.2, bf16[1,1,32,128,1024]{4,3,2,1,0:T(8,128)(2,1)} %hidden_hbm.1, f32[1,1,512,896]{3,2,1,0:T(8,128)} %master_hbm.1, ...), custom_call_target="tpu_custom_call" | custom-call | flops 7516192768 | bytes 16777216 | tf_op jit(solution)/shard_map/relay/pallas_call | solution.py:608
  110.8 0.5 slice.3
  111.9 0.0 copy-done
  111.9 2.5 %store.3 = (f32[1,1,512,896]{3,2,1,0:T(8,128)}, f32[1,1,512,896]{3,2,1,0:T(8,128)}, f32[1,1,512,896]{3,2,1,0:T(8,128)}) custom-call(f32[512,896]{1,0:T(8,128)S(1)} %get-tuple-element.35.refs_0_, f32[512,896]{1,0:T(8,128)S(1)} %get-tuple-element.36.refs_1_, f32[512,896]{1,0:T(8,128)S(1)} %get-tuple-element.37.refs_2_), custom_call_target="tpu_custom_call" | custom-call | tf_op jit(solution)/shard_map/store/pallas_call | solution.py:598
  (1 shorter events, 0.0 us)
Async XLA Ops:
  0.6 111.3 %copy-start = (f32[1,1,512,896]{3,2,1,0:T(8,128)S(1)}, f32[1,1,512,896]{3,2,1,0:T(8,128)}, u32[]{:S(2)}) copy-start(f32[1,1,512,896]{3,2,1,0:T(8,128)} %master_hbm.1) | copy-start | bytes 5505028

commit v5 on v4

--- a/solution.py
+++ b/solution.py
@@ -8,7 +8,8 @@
 EXPG = 4
 LANE = 128
 LAG = 3
-AHEAD = 3
+FIRST = 4
+BEHIND = 2
 CROSSING = 208
 MESH = pl.DeviceIdType.MESH
 
@@ -368,33 +369,40 @@
     def slab_cols(chunk, j):
         return pl.ds(pl.multiple_of(j * slab + chunk * LANE, LANE), LANE)
 
-    def send_own(chunk):
-        for step in range(split):
-            j = lax.rem(seat + step, split)
-            rows = jnp.dot(place[...], grad[:, slab_cols(chunk, j)], preferred_element_type=jnp.float32)
-            spread(chunk, 0, step, j, rows)
-
-    def packed_copy(chunk):
+    def packed_copy(chunk, j):
+        return pltpu.make_async_remote_copy(
+            src_ref=packed.at[chunk, j], dst_ref=packed_in.at[chunk, j],
+            send_sem=pack_send.at[chunk], recv_sem=pack_recv.at[chunk],
+            device_id=(pipe, partner), device_id_type=MESH,
+        )
+
+    def packed_all(chunk):
         return pltpu.make_async_remote_copy(
             src_ref=packed.at[chunk], dst_ref=packed_in.at[chunk],
             send_sem=pack_send.at[chunk], recv_sem=pack_recv.at[chunk],
             device_id=(pipe, partner), device_id_type=MESH,
         )
 
-    def send_packed(chunk):
-        for j in range(split):
-            rows = jnp.dot(pack[...], grad[:, slab_cols(chunk, j)], preferred_element_type=jnp.float32)
-            packed[chunk, j] = rows.astype(jnp.bfloat16)
-        packed_copy(chunk).start()
+    def slab_step(step, new, passed):
+        j = lax.rem(seat + step, split)
+        if passed is not None:
+            rows = jnp.dot(expand[...], packed_in[passed, j], preferred_element_type=jnp.float32)
+            spread(passed, 1, step, j, rows)
+        if new is not None:
+            rows = jnp.dot(place[...], grad[:, slab_cols(new, j)], preferred_element_type=jnp.float32)
+            spread(new, 0, step, j, rows)
+            rows = jnp.dot(pack[...], grad[:, slab_cols(new, j)], preferred_element_type=jnp.float32)
+            packed[new, j] = rows.astype(jnp.bfloat16)
+            packed_copy(new, j).start()
 
     def first_sends(chunk, carry):
-        send_own(chunk)
-        send_packed(chunk)
+        for step in range(split):
+            slab_step(step, chunk, None)
         return carry
 
     first_sends(0, 0)
     lax.fori_loop(1, plane, tell_plane, 0)
-    lax.fori_loop(1, chunks, first_sends, 0)
+    lax.fori_loop(1, FIRST, first_sends, 0)
 
     send_routes.wait_recv()
     their_places, their_ranks, _ = one_hots(routes_in[...], side)
@@ -402,17 +410,9 @@
         their_places, their_ranks, (((1,), (1,)), ((), ())), preferred_element_type=jnp.float32
     ).astype(jnp.bfloat16)
 
-    def relay(chunk):
-        packed_copy(chunk).wait_recv()
-        for step in range(split):
-            j = lax.rem(seat + step, split)
-            rows = jnp.dot(expand[...], packed_in[chunk, j], preferred_element_type=jnp.float32)
-            spread(chunk, 1, step, j, rows)
-
-    relay(0)
-
     turns = expert_count // group
-    for turn in range(turns):
+
+    def flip_turn(turn, carry):
         load_hidden(turn).wait()
 
         def flip(i, carry):
@@ -421,23 +421,12 @@
             return carry
 
         lax.fori_loop(0, group, flip, 0)
-        if turn + 2 < turns:
+
+        @pl.when(turn + 2 < turns)
+        def _():
             load_hidden(turn + 2).start()
 
-    over_all_plane.wait_recv()
-    over_pair[0] = jnp.max(over_plane[...], axis=0)
-    over_to_partner.start()
-
-    def relay_one(chunk, carry):
-        relay(chunk)
-        return carry
-
-    lax.fori_loop(1, AHEAD, relay_one, 0)
-
-    over_to_partner.wait_recv()
-    over_pipe[pipe] = jnp.maximum(over_pair[0], over_pair[1])
-    for copy in over_to_pipes:
-        copy.start()
+        return carry
 
     def code_copy(chunk):
         return pltpu.make_async_remote_copy(
@@ -477,10 +466,6 @@
         moment2[:, cols] = new_moment2
 
     def work(chunk, carry):
-        @pl.when(chunk + AHEAD < chunks)
-        def _():
-            relay(chunk + AHEAD)
-
         for kind in range(2):
             all_blocks(chunk, kind).wait_recv()
             local(chunk, kind).wait()
@@ -501,7 +486,43 @@
 
     for load in load_state:
         load.wait()
-    lax.fori_loop(0, chunks, work, 0)
+
+    def both(chunk, carry):
+        packed_all(chunk).wait_recv()
+        for step in range(split):
+            slab_step(step, chunk + FIRST, chunk)
+
+        @pl.when(chunk < BEHIND)
+        def _():
+            lax.fori_loop(chunk * turns // BEHIND, (chunk + 1) * turns // BEHIND, flip_turn, 0)
+
+        @pl.when(chunk >= BEHIND)
+        def _():
+            work(chunk - BEHIND, 0)
+
+        return carry
+
+    def passing(chunk, carry):
+        packed_all(chunk).wait_recv()
+        for step in range(split):
+            slab_step(step, None, chunk)
+        work(chunk - BEHIND, 0)
+        return carry
+
+    lax.fori_loop(0, chunks - FIRST, both, 0)
+
+    over_all_plane.wait_recv()
+    over_pair[0] = jnp.max(over_plane[...], axis=0)
+    over_to_partner.start()
+
+    lax.fori_loop(chunks - FIRST, chunks, passing, 0)
+
+    over_to_partner.wait_recv()
+    over_pipe[pipe] = jnp.maximum(over_pair[0], over_pair[1])
+    for copy in over_to_pipes:
+        copy.start()
+
+    lax.fori_loop(chunks - BEHIND, chunks, work, 0)
 
     def finish_rest(chunk, carry):
         finish(chunk)
@@ -519,7 +540,7 @@
     def drain(chunk, carry):
         for kind in range(2):
             all_blocks(chunk, kind).wait_send()
-        packed_copy(chunk).wait_send()
+        packed_all(chunk).wait_send()
         code_copy(chunk).wait_send()
         scale_copy(chunk).wait_send()
         return carry

time: 115 us -> 106 us (0.922)
  Pallas kernels: 113 us -> 102 us
    pallas_call x1, Pallas kernels: 110 us -> 99.7 us  [body(): pl.pallas_call(relay_kernel, out_shape=(state, state, state, jax.ShapeDty...]
where the time goes in v5:
time: 106 us; the launch traced here: 104 us
  Pallas kernels  102 us (96%)
  between operations  1.48 us (1%)
    pallas_call x1, Pallas kernels, body(): pl.pallas_call(relay_kernel, out_shape=(state, state, state, jax.ShapeDty...  99.7 us
    pallas_call x1, Pallas kernels, stored(): pl.pallas_call(store_kernel, out_shape=(shape, shape, shape), in_specs=[p...  2.46 us

profile of v5, /device:TPU:1, one launch (start us, length us, event | category | flops | bytes accessed | tf_op | source)
XLA Modules:
  0.0 104.4 jit_solution(5005306211549664895)
XLA Ops:
  0.6 0.0 copy-start
  0.6 99.7 %relay.1 = (f32[512,896]{1,0:T(8,128)S(1)}, f32[512,896]{1,0:T(8,128)S(1)}, f32[512,896]{1,0:T(8,128)S(1)}, s32[8,128]{1,0:T(8,128)S(1)}) custom-call(bf16[256,7168]{1,0:T(8,128)(2,1)} %grad_hbm.1, s32[1,256]{1,0:T(1,128)} %bitcast.2, bf16[1,1,32,128,1024]{4,3,2,1,0:T(8,128)(2,1)} %hidden_hbm.1, f32[1,1,512,896]{3,2,1,0:T(8,128)} %master_hbm.1, ...), custom_call_target="tpu_custom_call" | custom-call | flops 7516192768 | bytes 16777216 | tf_op jit(solution)/shard_map/relay/pallas_call | solution.py:629
  100.4 0.5 slice.3
  101.5 0.0 copy-done
  101.6 2.5 %store.3 = (f32[1,1,512,896]{3,2,1,0:T(8,128)}, f32[1,1,512,896]{3,2,1,0:T(8,128)}, f32[1,1,512,896]{3,2,1,0:T(8,128)}) custom-call(f32[512,896]{1,0:T(8,128)S(1)} %get-tuple-element.35.refs_0_, f32[512,896]{1,0:T(8,128)S(1)} %get-tuple-element.36.refs_1_, f32[512,896]{1,0:T(8,128)S(1)} %get-tuple-element.37.refs_2_), custom_call_target="tpu_custom_call" | custom-call | tf_op jit(solution)/shard_map/store/pallas_call | solution.py:619
  104.0 0.2 conditional.1
Async XLA Ops:
  0.6 100.9 %copy-start = (f32[1,1,512,896]{3,2,1,0:T(8,128)S(1)}, f32[1,1,512,896]{3,2,1,0:T(8,128)}, u32[]{:S(2)}) copy-start(f32[1,1,512,896]{3,2,1,0:T(8,128)} %master_hbm.1) | copy-start | bytes 5505028

commit v6 on v5

--- a/solution.py
+++ b/solution.py
@@ -8,7 +8,7 @@
 EXPG = 4
 LANE = 128
 LAG = 3
-FIRST = 4
+FIRST = 5
 BEHIND = 2
 CROSSING = 208
 MESH = pl.DeviceIdType.MESH
@@ -235,14 +235,10 @@
             hidden_hbm.at[0, 0, pl.ds(turn * group, group)], hidden.at[turn % 2], hidden_sem.at[turn % 2]
         )
 
-    load_hidden(0).start()
-    load_hidden(1).start()
     load_state = [
         pltpu.make_async_copy(src.at[0, 0], dst, load_sem.at[2 + i])
         for i, (src, dst) in enumerate(((master_hbm, master), (moment1_hbm, moment1), (moment2_hbm, moment2)))
     ]
-    for load in load_state:
-        load.start()
 
     barrier = pltpu.get_barrier_semaphore()
 
@@ -401,6 +397,10 @@
         return carry
 
     first_sends(0, 0)
+    load_hidden(0).start()
+    load_hidden(1).start()
+    for load in load_state:
+        load.start()
     lax.fori_loop(1, plane, tell_plane, 0)
     lax.fori_loop(1, FIRST, first_sends, 0)
 
@@ -453,29 +453,37 @@
         lax.fori_loop(0, half // tile, one, 0)
 
     def finish(chunk):
-        code_copy(chunk).wait_recv()
-        scale_copy(chunk).wait_recv()
-        summed = own[chunk] + code_in[chunk].astype(jnp.float32) * scale_in[chunk, 0:1, :]
         cols = pl.ds(pl.multiple_of(chunk * LANE, LANE), LANE)
-        new_moment1 = 0.9 * moment1[:, cols] + 0.1 * summed
-        new_moment2 = 0.95 * moment2[:, cols] + 0.05 * summed * summed
-        weight = master[:, cols]
-        update = new_moment1 / (1.0 - 0.9**10) / (jnp.sqrt(new_moment2 / (1.0 - 0.95**10)) + 1e-08)
-        master[:, cols] = weight - 0.2 * (update + 0.05 * weight)
-        moment1[:, cols] = new_moment1
-        moment2[:, cols] = new_moment2
+        for part in range(half // tile):
+            index = chunk * (half // tile) + part
+            code_copy(index).wait_recv()
+            scale_copy(index).wait_recv()
+            rows = slice(part * tile, (part + 1) * tile)
+            summed = own[chunk, rows] + code_in[index].astype(jnp.float32) * scale_in[index, 0:1, :]
+            new_moment1 = 0.9 * moment1[rows, cols] + 0.1 * summed
+            new_moment2 = 0.95 * moment2[rows, cols] + 0.05 * summed * summed
+            weight = master[rows, cols]
+            update = new_moment1 / (1.0 - 0.9**10) / (jnp.sqrt(new_moment2 / (1.0 - 0.95**10)) + 1e-08)
+            master[rows, cols] = weight - 0.2 * (update + 0.05 * weight)
+            moment1[rows, cols] = new_moment1
+            moment2[rows, cols] = new_moment2
 
     def work(chunk, carry):
         for kind in range(2):
             all_blocks(chunk, kind).wait_recv()
             local(chunk, kind).wait()
-        multiply(chunk, other_start, other)
-        part = other[...]
-        top = jnp.maximum(jnp.max(jnp.abs(part), axis=0, keepdims=True), 1e-30)
-        code[chunk] = jnp.floor(part * (32766.0 / top) + 0.5).astype(jnp.int16)
-        scale[chunk] = jnp.broadcast_to(top * (1.0 / 32766.0), scale.shape[1:])
-        code_copy(chunk).start()
-        scale_copy(chunk).start()
+        for part in range(half // tile):
+            index = chunk * (half // tile) + part
+            rows = pl.ds(pl.multiple_of(other_start + part * tile, tile), tile)
+            other[...] = jnp.dot(
+                hidden_t[rows, :], arrived[chunk].reshape(expert_count * cap, LANE), preferred_element_type=jnp.float32
+            )
+            value = other[...]
+            top = jnp.maximum(jnp.max(jnp.abs(value), axis=0, keepdims=True), 1e-30)
+            code[index] = jnp.floor(value * (32766.0 / top) + 0.5).astype(jnp.int16)
+            scale[index] = jnp.broadcast_to(top * (1.0 / 32766.0), scale.shape[1:])
+            code_copy(index).start()
+            scale_copy(index).start()
         multiply(chunk, own_start, own.at[chunk])
 
         @pl.when(chunk >= LAG)
@@ -531,7 +539,7 @@
     lax.fori_loop(chunks - LAG, chunks, finish_rest, 0)
 
     over_all_pipes.wait_recv()
-    over_out[...] = jnp.max(over_pipe[...], axis=0)
+    over_out[...] = jnp.max(over_pipe[...], axis=0)[0:1, 0:1]
     send_routes.wait_send()
     over_all_plane.wait_send()
     over_to_partner.wait_send()
@@ -541,8 +549,9 @@
         for kind in range(2):
             all_blocks(chunk, kind).wait_send()
         packed_all(chunk).wait_send()
-        code_copy(chunk).wait_send()
-        scale_copy(chunk).wait_send()
+        for part in range(half // tile):
+            code_copy(chunk * (half // tile) + part).wait_send()
+            scale_copy(chunk * (half // tile) + part).wait_send()
         return carry
 
     lax.fori_loop(0, chunks, drain, 0)
@@ -628,7 +637,7 @@
 
     *states, over = pl.pallas_call(
         relay_kernel,
-        out_shape=(state, state, state, jax.ShapeDtypeStruct((8, LANE), jnp.int32)),
+        out_shape=(state, state, state, jax.ShapeDtypeStruct((1, 1), jnp.int32)),
         in_specs=[pl.BlockSpec(memory_space=pl.ANY), pl.BlockSpec(memory_space=pltpu.HBM)]
         + [pl.BlockSpec(memory_space=pl.ANY)] * 4,
         out_specs=[pl.BlockSpec(memory_space=pltpu.VMEM)] * 4,
@@ -646,11 +655,11 @@
             pltpu.VMEM((2, expert_count // 8, cap, hid), bf16),
             pltpu.VMEM((hid, expert_count * cap), bf16),
             pltpu.VMEM((chunks, half, LANE), f32),
-            pltpu.VMEM((half, LANE), f32),
-            pltpu.VMEM((chunks, half, LANE), jnp.int16),
-            pltpu.VMEM((chunks, half, LANE), jnp.int16),
-            pltpu.VMEM((chunks, 8, LANE), f32),
-            pltpu.VMEM((chunks, 8, LANE), f32),
+            pltpu.VMEM((half // 2, LANE), f32),
+            pltpu.VMEM((2 * chunks, half // 2, LANE), jnp.int16),
+            pltpu.VMEM((2 * chunks, half // 2, LANE), jnp.int16),
+            pltpu.VMEM((2 * chunks, 8, LANE), f32),
+            pltpu.VMEM((2 * chunks, 8, LANE), f32),
             pltpu.VMEM((plane, 8, LANE), jnp.int32),
             pltpu.VMEM((2, 8, LANE), jnp.int32),
             pltpu.VMEM((lax.axis_size("pipe"), 8, LANE), jnp.int32),
@@ -663,7 +672,7 @@
             dma((2, chunks)),
             dma((2, chunks)),
             dma((2, chunks)),
-        ] + [dma((chunks,))] * 4,
+        ] + [dma((2 * chunks,))] * 4,
         compiler_params=pltpu.CompilerParams(
             collective_id=0, has_side_effects=True, vmem_limit_bytes=48 * 1024 * 1024
         ),

time: 106 us -> 104 us (0.981); the launches traced: 104 us -> 104 us
  no operation moved by 1% of the time
where the time goes in v6:
time: 104 us
  Pallas kernels  103 us (99%)
  between operations  1.44 us (1%)
    pallas_call x1, Pallas kernels, body(): pl.pallas_call(relay_kernel, out_shape=(state, state, state, jax.ShapeDty...  100 us
    pallas_call x1, Pallas kernels, stored(): pl.pallas_call(store_kernel, out_shape=(shape, shape, shape), in_specs=[p...  2.46 us

profile of v6, /device:TPU:1, one launch (start us, length us, event | category | flops | bytes accessed | tf_op | source)
XLA Modules:
  0.0 104.0 jit_solution(15756260386114630255)
XLA Ops:
  0.6 0.0 copy-start
  0.6 100.1 %relay.1 = (f32[512,896]{1,0:T(8,128)S(1)}, f32[512,896]{1,0:T(8,128)S(1)}, f32[512,896]{1,0:T(8,128)S(1)}, s32[1,1]{1,0:T(1,128)}) custom-call(bf16[256,7168]{1,0:T(8,128)(2,1)} %grad_hbm.1, s32[1,256]{1,0:T(1,128)} %bitcast.2, bf16[1,1,32,128,1024]{4,3,2,1,0:T(8,128)(2,1)} %hidden_hbm.1, f32[1,1,512,896]{3,2,1,0:T(8,128)} %master_hbm.1, ...), custom_call_target="tpu_custom_call" | custom-call | flops 7516192768 | bytes 16777216 | tf_op jit(solution)/shard_map/relay/pallas_call | solution.py:638
  101.4 0.0 copy-done
  101.4 2.5 %store.3 = (f32[1,1,512,896]{3,2,1,0:T(8,128)}, f32[1,1,512,896]{3,2,1,0:T(8,128)}, f32[1,1,512,896]{3,2,1,0:T(8,128)}) custom-call(f32[512,896]{1,0:T(8,128)S(1)} %get-tuple-element.35.refs_0_, f32[512,896]{1,0:T(8,128)S(1)} %get-tuple-element.36.refs_1_, f32[512,896]{1,0:T(8,128)S(1)} %get-tuple-element.37.refs_2_), custom_call_target="tpu_custom_call" | custom-call | tf_op jit(solution)/shard_map/store/pallas_call | solution.py:628
  (1 shorter events, 0.0 us)
Async XLA Ops:
  0.6 100.7 %copy-start = (f32[1,1,512,896]{3,2,1,0:T(8,128)S(1)}, f32[1,1,512,896]{3,2,1,0:T(8,128)}, u32[]{:S(2)}) copy-start(f32[1,1,512,896]{3,2,1,0:T(8,128)} %master_hbm.1) | copy-start | bytes 5505028

commit v7 on v6

--- a/solution.py
+++ b/solution.py
@@ -382,8 +382,9 @@
     def slab_step(step, new, passed):
         j = lax.rem(seat + step, split)
         if passed is not None:
-            rows = jnp.dot(expand[...], packed_in[passed, j], preferred_element_type=jnp.float32)
-            spread(passed, 1, step, j, rows)
+            far = lax.rem(seat + split - step, split)
+            rows = jnp.dot(expand[...], packed_in[passed, far], preferred_element_type=jnp.float32)
+            spread(passed, 1, step, far, rows)
         if new is not None:
             rows = jnp.dot(place[...], grad[:, slab_cols(new, j)], preferred_element_type=jnp.float32)
             spread(new, 0, step, j, rows)

time: 104 us -> 105 us (level); the launches traced: 104 us -> 104 us
  no operation moved by 1% of the time
where the time goes in v7:
time: 105 us; the launch traced here: 104 us
  Pallas kernels  102 us (97%)
  between operations  1.44 us (1%)
    pallas_call x1, Pallas kernels, body(): pl.pallas_call(relay_kernel, out_shape=(state, state, state, jax.ShapeDty...  99.7 us
    pallas_call x1, Pallas kernels, stored(): pl.pallas_call(store_kernel, out_shape=(shape, shape, shape), in_specs=[p...  2.46 us

profile of v7, /device:TPU:1, one launch (start us, length us, event | category | flops | bytes accessed | tf_op | source)
XLA Modules:
  0.0 103.6 jit_solution(3887872818677070456)
XLA Ops:
  0.6 0.0 copy-start
  0.6 99.7 %relay.1 = (f32[512,896]{1,0:T(8,128)S(1)}, f32[512,896]{1,0:T(8,128)S(1)}, f32[512,896]{1,0:T(8,128)S(1)}, s32[1,1]{1,0:T(1,128)}) custom-call(bf16[256,7168]{1,0:T(8,128)(2,1)} %grad_hbm.1, s32[1,256]{1,0:T(1,128)} %bitcast.2, bf16[1,1,32,128,1024]{4,3,2,1,0:T(8,128)(2,1)} %hidden_hbm.1, f32[1,1,512,896]{3,2,1,0:T(8,128)} %master_hbm.1, ...), custom_call_target="tpu_custom_call" | custom-call | flops 7516192768 | bytes 16777216 | tf_op jit(solution)/shard_map/relay/pallas_call | solution.py:639
  101.0 0.0 copy-done
  101.0 2.5 %store.3 = (f32[1,1,512,896]{3,2,1,0:T(8,128)}, f32[1,1,512,896]{3,2,1,0:T(8,128)}, f32[1,1,512,896]{3,2,1,0:T(8,128)}) custom-call(f32[512,896]{1,0:T(8,128)S(1)} %get-tuple-element.35.refs_0_, f32[512,896]{1,0:T(8,128)S(1)} %get-tuple-element.36.refs_1_, f32[512,896]{1,0:T(8,128)S(1)} %get-tuple-element.37.refs_2_), custom_call_target="tpu_custom_call" | custom-call | tf_op jit(solution)/shard_map/store/pallas_call | solution.py:629
  (1 shorter events, 0.0 us)
Async XLA Ops:
  0.6 100.4 %copy-start = (f32[1,1,512,896]{3,2,1,0:T(8,128)S(1)}, f32[1,1,512,896]{3,2,1,0:T(8,128)}, u32[]{:S(2)}) copy-start(f32[1,1,512,896]{3,2,1,0:T(8,128)} %master_hbm.1) | copy-start | bytes 5505028
